TPU v7x, 32 devices: a whole 2x2x4 slice. The times are simulated.
32 devices in a mesh: ens: 2 (over x), region: 16 (over z, y, core).
Axes of the slice: x: 2, y: 2, z: 4, core: 2. Of those that a mesh axis runs over, the one named last changes fastest.
Arguments:
- velocity_start: float32 [2, 20, 16384], P(None, None, ('ens', 'region')), parts along dimension 2, may hold values from -6 to 6
- forcing: float32 [2, 20, 16384], P(None, None, ('ens', 'region')), parts along dimension 2, may hold values from -6 to 6
- rate_factor: float32 [20, 16384], P(None, ('ens', 'region')), parts along dimension 1, may hold values from 0.5 to 2
- basal_drag: float32 [8192], P('region'), may hold values from 0.1 to 10
- edge_weight: float32 [6, 8192], P(None, 'region'), may hold values from 0.3 to 1.5
- nbr_local: int32 [6, 8192], P(None, 'region'), may hold values from 0 to 575, as said below
- send_list: int32 [2, 512], P(None, 'region'), may hold values from 0 to 511, as said below
- ice_mask: int32 [8192], P('region'), may hold values from 0 to 1, as said below
Outputs:
- velocity: float32 [2, 20, 16384], P(None, None, ('ens', 'region')), parts along dimension 2
- newton_residual: float32 [2, 20, 16384], P(None, None, ('ens', 'region')), parts along dimension 2
There are 2 independent parts, one for each index of `ens`. A program takes and returns all parts, laid end to end along the dimension named above; an argument that names none is the same for every part. Nothing has to cross between parts.
Inputs may be any that keep to these rules, and one draw needn't show every extreme that they name: `nbr_local`: column c of a partition (c = 0, ..., 511) has its neighbours within 32 positions of its own position 32 + c in the extended list, so only columns near a partition's ends reach the halo blocks. `send_list`: a partition sends each of its first 32 columns once to the lower neighbour and each of its last 32 columns once to the upper one. `ice_mask`: each partition holds between a quarter of 512 and 384 ice columns, and some partition holds exactly 384.
All inputs are finite; a program needn't handle non-finite values.
Results may differ from a plain program's by a relative error of at most 0.0003.
Values sent between devices are 32-bit elements; how exact they have to be, the bound alone decides.
A program may use at most 64 MiB of HBM per device.

v0:
```python
import jax
import jax.numpy as jnp
from jax import lax
from jax.sharding import PartitionSpec as P

L = 20
NB = 6
M = 4
SWEEPS = 3


def with_halo(value, sides, width):
    for axis, dim in sides:
        peers, length = (lax.axis_size(axis), value.shape[dim])
        up = [(i, (i + 1) % peers) for i in range(peers - 1)]
        down = [(j, i) for i, j in up]
        last = lax.slice_in_dim(value, length - width, length, axis=dim)
        first = lax.slice_in_dim(value, 0, width, axis=dim)
        before = lax.ppermute(last, axis, up)
        after = lax.ppermute(first, axis, down)
        value = jnp.concatenate([before, value, after], axis=dim)
    return value


def viscosity_of(velocity_start, rate_factor):
    steps_up = velocity_start[:, 1:] - velocity_start[:, :-1]
    steps_up = jnp.concatenate([steps_up, jnp.zeros_like(velocity_start[:, :1])], axis=1)
    shear = jnp.sum(steps_up * steps_up, axis=0)
    return rate_factor * (1.0 + shear) ** (-1.0 / 3.0)


def local_terms(field, viscosity, face_visc, weight_total, basal_drag):
    flux = face_visc * (field[:, 1:] - field[:, :-1])
    blank = jnp.zeros_like(field[:, :1])
    vertical = -4.0 * (
        jnp.concatenate([flux, blank], axis=1) - jnp.concatenate([blank, flux], axis=1)
    )
    bed = jnp.concatenate(
        [(basal_drag * field[:, 0])[:, None], jnp.zeros_like(field[:, 1:])], axis=1
    )
    return vertical + (weight_total + 1.0) * viscosity * field + bed


def band_terms(viscosity, face_visc, weight_total, basal_drag, iced):
    blank = jnp.zeros_like(viscosity[:1])
    upper = jnp.concatenate([-4.0 * face_visc, blank], axis=0)
    lower = jnp.concatenate([blank, -4.0 * face_visc], axis=0)
    bottom = jnp.concatenate([basal_drag[None], jnp.zeros_like(viscosity[1:])], axis=0)
    middle = -upper - lower + (weight_total + 1.0) * viscosity + bottom
    return (lower * iced, iced * middle + (1.0 - iced), upper * iced)


def thomas(lower, middle, upper, right):
    layers = middle.shape[0]
    primes = [upper[0] / middle[0]]
    values = [right[:, 0] / middle[0]]
    for layer in range(1, layers):
        denom = middle[layer] - lower[layer] * primes[layer - 1]
        primes.append(upper[layer] / denom)
        values.append((right[:, layer] - lower[layer] * values[layer - 1]) / denom)
    solved = [values[layers - 1]]
    for layer in range(layers - 2, -1, -1):
        solved.insert(0, values[layer] - primes[layer] * solved[0])
    return jnp.stack(solved, axis=1)


def outgoing(field, send_list):
    return jnp.stack(
        [jnp.take(field, send_list[0], axis=-1), jnp.take(field, send_list[1], axis=-1)], axis=0
    )


def with_rims(field, arrived):
    return jnp.concatenate([arrived[0], field, arrived[3]], axis=-1)


def body(
    velocity_start, forcing, rate_factor, basal_drag, edge_weight, nbr_local, send_list, ice_mask
):
    highest = lax.Precision.HIGHEST
    iced = ice_mask.astype(jnp.float32)
    viscosity = viscosity_of(velocity_start, rate_factor)
    face_visc = 0.5 * (viscosity[:-1] + viscosity[1:])
    weight_total = jnp.sum(edge_weight, axis=0)

    def near_sum(extended):
        total = edge_weight[0] * jnp.take(extended, nbr_local[0], axis=-1)
        for which in range(1, NB):
            total = total + edge_weight[which] * jnp.take(extended, nbr_local[which], axis=-1)
        return total

    def apply_op(field):
        weighted = iced * viscosity * field
        arrived = with_halo(outgoing(weighted, send_list), (("region", 0),), 1)
        near = near_sum(with_rims(weighted, arrived))
        inner = local_terms(field, viscosity, face_visc, weight_total, basal_drag)
        return iced * (inner - near) + (1.0 - iced) * field

    lower, middle, upper = band_terms(viscosity, face_visc, weight_total, basal_drag, iced)
    mean_visc = jnp.mean(viscosity, axis=0)
    coarse_diag = iced * (basal_drag / L + (weight_total + 1.0) * mean_visc) + (1.0 - iced)
    newton_residual = apply_op(velocity_start) - iced * forcing
    start_resid = -newton_residual
    beta_zero = jnp.sqrt(lax.psum(jnp.sum(start_resid * start_resid), "region") + 1e-12)
    basis = [start_resid / beta_zero]
    directions = []
    hessen = jnp.zeros((M + 1, M), jnp.float32)
    for inner_step in range(M):
        precondition_right = basis[inner_step]
        smooth = thomas(lower, middle, upper, precondition_right)
        precondition_weighted = iced * viscosity * smooth
        precondition_arrived = with_halo(
            outgoing(precondition_weighted, send_list), (("region", 0),), 1
        )
        precondition_near = near_sum(with_rims(precondition_weighted, precondition_arrived))
        precondition_inner = local_terms(smooth, viscosity, face_visc, weight_total, basal_drag)
        restricted = jnp.mean(
            precondition_right
            - (iced * (precondition_inner - precondition_near) + (1.0 - iced) * smooth),
            axis=1,
        )
        correction = 0.8 * restricted / coarse_diag
        for sweep in range(SWEEPS - 1):
            coarse_weighted = iced * mean_visc * correction
            coarse_arrived = with_halo(outgoing(coarse_weighted, send_list), (("region", 0),), 1)
            coarse_near = near_sum(with_rims(coarse_weighted, coarse_arrived))
            coarse_inner = (
                weight_total + 1.0
            ) * mean_visc * correction + basal_drag * correction / L
            correction = (
                correction
                + 0.8
                * (restricted - (iced * (coarse_inner - coarse_near) + (1.0 - iced) * correction))
                / coarse_diag
            )
        direction = smooth + correction[:, None, :]
        image = apply_op(direction)
        stacked = jnp.stack(basis)
        local_proj = jnp.einsum("jabc,abc->j", stacked, image, precision=highest)
        proj = lax.psum(local_proj, "region")
        image = image - jnp.einsum("j,jabc->abc", proj, stacked, precision=highest)
        length = jnp.sqrt(lax.psum(jnp.sum(image * image), "region") + 1e-12)
        hessen = hessen.at[: inner_step + 1, inner_step].set(proj)
        hessen = hessen.at[inner_step + 1, inner_step].set(length)
        basis.append(image / length)
        directions.append(direction)
    gram = jnp.dot(hessen.T, hessen, precision=highest)
    factor = jnp.linalg.cholesky(gram)
    coeffs = jax.scipy.linalg.cho_solve((factor, True), beta_zero * hessen[0])
    update = jnp.einsum("j,jabc->abc", coeffs, jnp.stack(directions), precision=highest)
    return (velocity_start + update, newton_residual)


def solution(mesh):
    in_specs = (
        P(None, None, ("ens", "region")),
        P(None, None, ("ens", "region")),
        P(None, ("ens", "region")),
        P("region"),
        P(None, "region"),
        P(None, "region"),
        P(None, "region"),
        P("region"),
    )
    out_specs = (P(None, None, ("ens", "region")), P(None, None, ("ens", "region")))
    return jax.shard_map(body, mesh=mesh, in_specs=in_specs, out_specs=out_specs, check_vma=False)
```

profile of v0, /device:TPU:0, one launch (start us, length us, event | category | flops | bytes accessed | tf_op | source)
XLA Modules:
  0.0 771.1 jit_solution(14104970617060497298)
XLA Ops:
  12.8 3.0 collective-permute-start
  21.4 3.7 slice_subtract_fusion.1
  49.0 35.1 %psum.63 = f32[]{:T(128)} all-reduce(f32[]{:T(128)} %get-tuple-element.423), channel_id=1, replica_groups=mesh['ens'=2,'region'=16] {'region'}, use_global_device_ids=true, to_apply=%region_3.6 | all-reduce | flops 1 | bytes 8 | tf_op jit(solution)/shard_map/psum | solution.py:104
  96.4 2.7 gather_fusion.15
  119.6 5.2 collective-permute-start.4
  138.4 4.3 collective-permute-start.6
  142.8 3.5 copy.12178
  146.3 3.9 copy.12309
  150.3 3.3 copy.12179
  164.4 3.7 collective-permute-start.8
  191.0 35.4 %psum.64 = f32[1]{0:T(128)} all-reduce(f32[1]{0:T(128)} %bitcast.75), channel_id=1, replica_groups=mesh['ens'=2,'region'=16] {'region'}, use_global_device_ids=true, to_apply=%region_6.0 | all-reduce | flops 1 | bytes 8 | tf_op jit(solution)/shard_map/psum | solution.py:140
  228.5 30.3 %psum.65 = f32[]{:T(128)} all-reduce(f32[]{:T(128)} %multiply_reduce_fusion.3), channel_id=1, replica_groups=mesh['ens'=2,'region'=16] {'region'}, use_global_device_ids=true, to_apply=%region_8.0 | all-reduce | flops 1 | bytes 8 | tf_op jit(solution)/shard_map/psum | solution.py:142
  267.8 3.0 collective-permute-start.10
  295.2 3.8 collective-permute-start.12
  313.5 4.9 collective-permute-start.14
  330.8 4.2 collective-permute-start.16
  358.1 31.9 %psum.66 = f32[2]{0:T(128)S(1)} all-reduce(f32[2]{0:T(128)S(1)} %convolution_bitcast_fusion.4), channel_id=1, replica_groups=mesh['ens'=2,'region'=16] {'region'}, use_global_device_ids=true, to_apply=%region_11.16 | all-reduce | flops 2 | bytes 16 | tf_op jit(solution)/shard_map/psum | solution.py:140
  393.1 30.1 %psum.67 = f32[]{:T(128)} all-reduce(f32[]{:T(128)} %multiply_reduce_fusion.2), channel_id=1, replica_groups=mesh['ens'=2,'region'=16] {'region'}, use_global_device_ids=true, to_apply=%region_13.18 | all-reduce | flops 1 | bytes 8 | tf_op jit(solution)/shard_map/psum | solution.py:142
  431.7 3.4 collective-permute-start.18
  435.2 3.2 broadcast_select_fusion.2
  462.0 3.6 collective-permute-start.20
  478.9 4.3 collective-permute-start.22
  498.4 4.8 collective-permute-start.24
  525.4 31.3 %psum.68 = f32[3]{0:T(128)S(1)} all-reduce(f32[3]{0:T(128)S(1)} %convolution_bitcast_fusion.3), channel_id=1, replica_groups=mesh['ens'=2,'region'=16] {'region'}, use_global_device_ids=true, to_apply=%region_16.21 | all-reduce | flops 3 | bytes 24 | tf_op jit(solution)/shard_map/psum | solution.py:140
  558.9 30.1 %psum.69 = f32[]{:T(128)} all-reduce(f32[]{:T(128)} %multiply_reduce_fusion.1), channel_id=1, replica_groups=mesh['ens'=2,'region'=16] {'region'}, use_global_device_ids=true, to_apply=%region_18.23 | all-reduce | flops 1 | bytes 8 | tf_op jit(solution)/shard_map/psum | solution.py:142
  597.4 3.2 collective-permute-start.26
  624.9 3.7 collective-permute-start.28
  646.2 4.9 collective-permute-start.30
  665.7 4.5 collective-permute-start.32
  692.8 31.3 %psum.70 = f32[4]{0:T(128)S(1)} all-reduce(f32[4]{0:T(128)S(1)} %convolution_bitcast_fusion.2), channel_id=1, replica_groups=mesh['ens'=2,'region'=16] {'region'}, use_global_device_ids=true, to_apply=%region_21.26 | all-reduce | flops 4 | bytes 32 | tf_op jit(solution)/shard_map/psum | solution.py:140
  726.7 30.1 %psum.71 = f32[]{:T(128)} all-reduce(f32[]{:T(128)} %fusion.16), channel_id=1, replica_groups=mesh['ens'=2,'region'=16] {'region'}, use_global_device_ids=true, to_apply=%region_23.28 | all-reduce | flops 1 | bytes 8 | tf_op jit(solution)/shard_map/psum | solution.py:142
  757.5 2.6 broadcast_select_fusion
  (868 shorter events, 390.0 us)
Async XLA Ops:
  10.0 23.5 %collective-permute-start.1 = (f32[1,2,20,32]{2,1,3,0:T(2,128)S(1)}, f32[1,2,20,32]{2,1,3,0:T(2,128)S(1)}, u32[]{:S(2)}, u32[]{:S(2)}) collective-permute-start(f32[1,2,20,32]{2,1,3,0:T(2,128)S(1)} %select_bitcast_fusion.16), channel_id=1, source_target_pairs={{1,0},{2,1},{3,2},{4,3},{5,4},{6,5},{7,6},{8,7},{9,8},{10,9},{11,1... | collective-permute-start | bytes 15368 | tf_op jit(solution)/shard_map/ppermute | solution.py:20
  12.8 20.9 %collective-permute-start = (f32[1,2,20,32]{2,1,3,0:T(2,128)S(1)}, f32[1,2,20,32]{2,1,3,0:T(2,128)S(1)}, u32[]{:S(2)}, u32[]{:S(2)}) collective-permute-start(f32[1,2,20,32]{2,1,3,0:T(2,128)S(1)} %select_bitcast_fusion.17), channel_id=1, source_target_pairs={{0,1},{1,2},{2,3},{3,4},{4,5},{5,6},{6,7},{7,8},{8,9},{9,10},{10,1... | collective-permute-start | bytes 15368 | tf_op jit(solution)/shard_map/ppermute | solution.py:19
  92.2 3.5 collective-permute-start.3
  118.3 7.8 %collective-permute-start.5 = (f32[1,2,32]{2,1,0:T(2,128)S(1)}, f32[1,2,32]{2,1,0:T(2,128)S(1)}, u32[]{:S(2)}, u32[]{:S(2)}) collective-permute-start(f32[1,2,32]{2,1,0:T(2,128)S(1)} %bitcast.1484), channel_id=1, source_target_pairs={{1,0},{2,1},{3,2},{4,3},{5,4},{6,5},{7,6},{8,7},{9,8},{10,9},{11,1... | collective-permute-start | bytes 776 | tf_op jit(solution)/shard_map/ppermute | solution.py:20
  119.6 6.5 collective-permute-start.4
  137.1 16.4 %collective-permute-start.7 = (f32[1,2,32]{2,1,0:T(2,128)S(1)}, f32[1,2,32]{2,1,0:T(2,128)S(1)}, u32[]{:S(2)}, u32[]{:S(2)}) collective-permute-start(f32[1,2,32]{2,1,0:T(2,128)S(1)} %bitcast.1480), channel_id=1, source_target_pairs={{1,0},{2,1},{3,2},{4,3},{5,4},{6,5},{7,6},{8,7},{9,8},{10,9},{11,1... | collective-permute-start | bytes 776 | tf_op jit(solution)/shard_map/ppermute | solution.py:20
  138.4 15.2 %collective-permute-start.6 = (f32[1,2,32]{2,1,0:T(2,128)S(1)}, f32[1,2,32]{2,1,0:T(2,128)S(1)}, u32[]{:S(2)}, u32[]{:S(2)}) collective-permute-start(f32[1,2,32]{2,1,0:T(2,128)S(1)} %bitcast.1472), channel_id=1, source_target_pairs={{0,1},{1,2},{2,3},{3,4},{4,5},{5,6},{6,7},{7,8},{8,9},{9,10},{10,1... | collective-permute-start | bytes 776 | tf_op jit(solution)/shard_map/ppermute | solution.py:19
  164.4 5.6 collective-permute-start.8
  266.5 4.4 collective-permute-start.11
  267.8 3.9 collective-permute-start.10
  293.9 7.2 collective-permute-start.13
  295.2 5.9 collective-permute-start.12
  312.2 6.3 collective-permute-start.15
  313.5 5.7 collective-permute-start.14
  329.5 6.1 collective-permute-start.17
  330.8 5.0 collective-permute-start.16
  430.4 8.0 %collective-permute-start.19 = (f32[1,2,20,32]{2,1,3,0:T(2,128)S(1)}, f32[1,2,20,32]{2,1,3,0:T(2,128)S(1)}, u32[]{:S(2)}, u32[]{:S(2)}) collective-permute-start(f32[1,2,20,32]{2,1,3,0:T(2,128)S(1)} %select_bitcast_fusion.6), channel_id=1, source_target_pairs={{1,0},{2,1},{3,2},{4,3},{5,4},{6,5},{7,6},{8,7},{9,8},{10,9},{11,1... | collective-permute-start | bytes 15368 | tf_op jit(solution)/shard_map/ppermute | solution.py:20
  431.7 6.8 collective-permute-start.18
  460.7 5.8 collective-permute-start.21
  462.0 4.5 collective-permute-start.20
  477.6 9.4 %collective-permute-start.23 = (f32[1,2,32]{2,1,0:T(2,128)S(1)}, f32[1,2,32]{2,1,0:T(2,128)S(1)}, u32[]{:S(2)}, u32[]{:S(2)}) collective-permute-start(f32[1,2,32]{2,1,0:T(2,128)S(1)} %bitcast.1477), channel_id=1, source_target_pairs={{1,0},{2,1},{3,2},{4,3},{5,4},{6,5},{7,6},{8,7},{9,8},{10,9},{11,1... | collective-permute-start | bytes 776 | tf_op jit(solution)/shard_map/ppermute | solution.py:20
  478.9 8.1 %collective-permute-start.22 = (f32[1,2,32]{2,1,0:T(2,128)S(1)}, f32[1,2,32]{2,1,0:T(2,128)S(1)}, u32[]{:S(2)}, u32[]{:S(2)}) collective-permute-start(f32[1,2,32]{2,1,0:T(2,128)S(1)} %bitcast.1469), channel_id=1, source_target_pairs={{0,1},{1,2},{2,3},{3,4},{4,5},{5,6},{6,7},{7,8},{8,9},{9,10},{10,1... | collective-permute-start | bytes 776 | tf_op jit(solution)/shard_map/ppermute | solution.py:19
  497.1 6.8 collective-permute-start.25
  498.4 5.5 collective-permute-start.24
  596.1 4.6 collective-permute-start.27
  597.4 3.9 collective-permute-start.26
  623.6 10.2 %collective-permute-start.29 = (f32[1,2,32]{2,1,0:T(2,128)S(1)}, f32[1,2,32]{2,1,0:T(2,128)S(1)}, u32[]{:S(2)}, u32[]{:S(2)}) collective-permute-start(f32[1,2,32]{2,1,0:T(2,128)S(1)} %bitcast.1478), channel_id=1, source_target_pairs={{1,0},{2,1},{3,2},{4,3},{5,4},{6,5},{7,6},{8,7},{9,8},{10,9},{11,1... | collective-permute-start | bytes 776 | tf_op jit(solution)/shard_map/ppermute | solution.py:20
  624.9 8.9 %collective-permute-start.28 = (f32[1,2,32]{2,1,0:T(2,128)S(1)}, f32[1,2,32]{2,1,0:T(2,128)S(1)}, u32[]{:S(2)}, u32[]{:S(2)}) collective-permute-start(f32[1,2,32]{2,1,0:T(2,128)S(1)} %bitcast.1470), channel_id=1, source_target_pairs={{0,1},{1,2},{2,3},{3,4},{4,5},{5,6},{6,7},{7,8},{8,9},{9,10},{10,1... | collective-permute-start | bytes 776 | tf_op jit(solution)/shard_map/ppermute | solution.py:19
  644.9 8.2 %collective-permute-start.31 = (f32[1,2,32]{2,1,0:T(2,128)S(1)}, f32[1,2,32]{2,1,0:T(2,128)S(1)}, u32[]{:S(2)}, u32[]{:S(2)}) collective-permute-start(f32[1,2,32]{2,1,0:T(2,128)S(1)} %bitcast.1479), channel_id=1, source_target_pairs={{1,0},{2,1},{3,2},{4,3},{5,4},{6,5},{7,6},{8,7},{9,8},{10,9},{11,1... | collective-permute-start | bytes 776 | tf_op jit(solution)/shard_map/ppermute | solution.py:20
  646.2 6.9 collective-permute-start.30
  664.4 6.4 collective-permute-start.33
  665.7 5.2 collective-permute-start.32
  (75 other events, 3010.0 us)
where the time goes:
time: 784 us; the launch traced here: 771 us
  blocking collectives  286 us (36%)
  local copies, waits for them, and re-layouts  278 us (35%)
  other arithmetic  92.6 us (12%)
  starting transfers between devices  87.8 us (11%)
  matrix products  13.8 us (2%)
  between operations  8 us (1%)
    gather x170, local copies, waits for them, and re-layouts, near_sum(): jnp.take(extended, nbr_local[which], axis=-1)  172 us
    psum x4, blocking collectives, body(): proj = lax.psum(local_proj, 'region')  130 us
    psum x4, blocking collectives, body(): length = jnp.sqrt(lax.psum(jnp.sum(image * image), 'region') + 1e-12)  121 us
    ppermute x17, starting transfers between devices, with_halo(): before = lax.ppermute(last, axis, up)  65.9 us
    psum x1, blocking collectives, body(): lax.psum(jnp.sum(start_resid * start_resid), 'region') + 1e-12  35.1 us
    gather x34, local copies, waits for them, and re-layouts, near_sum(): total = edge_weight[0] * jnp.take(extended, nbr_local[0], axis=-1)  31.4 us
    ppermute x17, starting transfers between devices, with_halo(): after = lax.ppermute(first, axis, down)  21.9 us
  transfers between devices with their start and end apart: 34, of which 6 were waited for; matrix products, arithmetic and copies ran while one was open for 7% of the time, Pallas kernels for 0%

commit v1 on v0

v1 whole, which is shorter than its diff:
```python
import functools

import jax
import jax.numpy as jnp
from jax import lax
from jax.experimental import pallas as pl
from jax.experimental.pallas import tpu as pltpu
from jax.sharding import PartitionSpec as P

M = 4
NB = 6
REACH = 32
LANES = 128
MESH = pl.DeviceIdType.MESH


def pick(value, index):
    return jnp.take_along_axis(value, index, axis=1, mode="promise_in_bounds")


def kernel(
    n, layers,
    vel, frc, rate, drag, ew, nbr, send, mask, vel_out, res_out,
    v2, f2, iv2, inv2, li2, pr2, td2, x2, h2, ivh2, w2, s2, u2, z2, ewf, idxf, ewc, nbc, tab,
    msg, got, smsg, sgot, imsg, igot, red,
    hs, hr, ss, sr, is_, ir, rs, rr,
):
    me = lax.axis_index("region")
    barrier = pltpu.get_barrier_semaphore()
    for off in range(1, n):
        pl.semaphore_signal(
            barrier, inc=1, device_id={"region": lax.rem(me + off, n)}, device_id_type=MESH
        )
    has_low, has_up = me > 0, me < n - 1
    sub = lax.broadcasted_iota(jnp.int32, (8, LANES), 0)
    lane = lax.broadcasted_iota(jnp.int32, (8, LANES), 1)
    tile = sub & 3
    width = 4 * LANES
    tail = lane >= LANES - REACH
    zero = jnp.zeros((8, LANES), jnp.float32)

    def row(ref, layer):
        return ref[pl.ds(8 * layer, 8), :]

    def put(ref, layer, value):
        ref[pl.ds(8 * layer, 8), :] = value

    def spread(ref, first, count, value):
        ref[pl.ds(first, count, stride=8), :] = value

    def gathered(ref, first, count):
        return ref[pl.ds(first, count, stride=8), :]

    for side, at, line in ((0, 0, 0), (1, 3, 1)):
        imsg[side, 0:NB, :] = nbr[:, at * LANES:(at + 1) * LANES]
        imsg[side, NB:8, :] = jnp.zeros((2, LANES), jnp.int32)
        imsg[side, NB:NB + 1, 0:REACH] = send[line:line + 1, :]

    for c in range(2):
        for t in range(4):
            cols = slice(t * LANES, (t + 1) * LANES)
            spread(v2, 4 * c + t, layers, vel[c, :, cols])
            spread(f2, 4 * c + t, layers, frc[c, :, cols])
            spread(iv2, 4 * c + t, layers, rate[:, cols])
            spread(ewf, 4 * c + t, NB, ew[:, cols])
    for k in range(NB):
        put(ewc, k, zero)
        put(nbc, k, jnp.zeros((8, LANES), jnp.int32))
    for t in range(4):
        cols = slice(t * LANES, (t + 1) * LANES)
        spread(ewc, 1 + t, NB, ew[:, cols])
        spread(nbc, 1 + t, NB, nbr[:, cols])
    ice4 = mask[...].astype(jnp.float32)
    iced = jnp.concatenate([ice4, ice4], axis=0)
    drag4 = drag[...]
    bed = jnp.concatenate([drag4, drag4], axis=0)
    h2[...] = jnp.zeros_like(h2)
    ivh2[...] = jnp.zeros_like(ivh2)

    total = row(ewf, 0)
    for k in range(1, NB):
        total = total + row(ewf, k)
    here = row(v2, 0)
    mean = zero
    for l in range(layers):
        if l < layers - 1:
            above = row(v2, l + 1)
            step = above - here
            square = step * step
            shear = square + pltpu.roll(square, 4, 0)
            here = above
            visc = row(iv2, l) * jnp.exp(jnp.log(1.0 + shear) * (-1.0 / 3.0))
        else:
            visc = row(iv2, l)
        mean = mean + visc
        put(iv2, l, visc)
    mean = mean * (1.0 / layers)
    factor = iced * (total + 1.0)
    other = 1.0 - iced
    coarse_diag = factor * mean + iced * (bed * (1.0 / layers)) + other
    put(s2, 0, 0.8 * iced / coarse_diag)
    put(s2, 1, iced * mean)
    below = zero
    last = zero
    prior = zero
    for l in range(layers):
        visc = row(iv2, l)
        diag = factor * visc + other
        if l == 0:
            diag = diag + iced * bed
        put(td2, l, diag)
        if l < layers - 1:
            face = iced * (2.0 * (visc + row(iv2, l + 1)))
        else:
            face = zero
        inverse = 1.0 / (diag + face + below - below * prior)
        put(inv2, l, inverse)
        put(li2, l, below * inverse)
        prior = face * inverse
        put(pr2, l, prior)
        value = row(v2, l)
        image = diag * value - iced * row(f2, l)
        if l < layers - 1:
            flux = face * (row(v2, l + 1) - value)
            image = image - flux
        else:
            flux = zero
        put(w2, l, image + last)
        last = flux
        below = face
    for l in range(layers):
        scaled = iced * row(iv2, l)
        put(iv2, l, scaled)
        put(x2, l, scaled * row(v2, l))
    for side, s in ((0, 0), (1, 3)):
        smsg[side, 0:layers, :] = gathered(x2, s, layers)
        smsg[side, 24:24 + layers, :] = gathered(x2, s + 4, layers)
        smsg[side, 48:48 + layers, :] = gathered(iv2, s, layers)
        smsg[side, 72:74, :] = gathered(s2, s, 2)
        smsg[side, 74:80, :] = ew[:, s * LANES:(s + 1) * LANES]

    def exchange(parts):
        low, up = me - 1, me + 1

        def copies(side):
            peer = low if side == 0 else up
            return [
                pltpu.make_async_remote_copy(
                    src_ref=src.at[side], dst_ref=dst.at[1 - side],
                    send_sem=ssem.at[side], recv_sem=rsem.at[1 - side],
                    device_id={"region": peer}, device_id_type=MESH,
                )
                for src, dst, ssem, rsem in parts
            ]

        def arrivals(side):
            peer = low if side == 0 else up
            return [
                pltpu.make_async_remote_copy(
                    src_ref=src.at[1 - side], dst_ref=dst.at[side],
                    send_sem=ssem.at[1 - side], recv_sem=rsem.at[side],
                    device_id={"region": peer}, device_id_type=MESH,
                )
                for src, dst, ssem, rsem in parts
            ]

        @pl.when(has_low)
        def _():
            for copy in copies(0):
                copy.start()

        @pl.when(has_up)
        def _():
            for copy in copies(1):
                copy.start()

        def finish(unpack):
            for side, there in ((0, has_low), (1, has_up)):
                @pl.when(there)
                def _():
                    for copy in arrivals(side):
                        copy.wait_recv()
                    unpack(side)

            for side, there in ((0, has_low), (1, has_up)):
                @pl.when(there)
                def _():
                    for copy in copies(side):
                        copy.wait_send()

        return finish

    pl.semaphore_wait(barrier, n - 1)
    finish = exchange([(imsg, igot, is_, ir), (smsg, sgot, ss, sr)])
    put(tab, 0, jnp.full((8, LANES), width - REACH, jnp.int32))
    put(tab, 1, jnp.zeros((8, LANES), jnp.int32))

    tab[5:6, :] = imsg[1, NB:NB + 1, :]
    tab[8:9, :] = imsg[0, NB:NB + 1, :]
    h3 = s2.at[pl.ds(16, 16)]
    h3[...] = jnp.zeros((16, LANES), jnp.float32)

    def unpack_first(side):
        s = 0 if side == 0 else 3
        place = 0 if side == 0 else 5
        spread(h2, s, layers, sgot[side, 0:layers, :])
        spread(h2, s + 4, layers, sgot[side, 24:24 + layers, :])
        spread(ivh2, s, layers, sgot[side, 48:48 + layers, :])
        spread(ivh2, s + 4, layers, sgot[side, 48:48 + layers, :])
        spread(h3, place, 2, sgot[side, 72:74, :])
        spread(ewc, place, NB, sgot[side, 74:80, :])
        spread(nbc, place, NB, igot[side, 0:NB, :])
        if side == 0:
            tab[1:2, :] = igot[0, NB:NB + 1, :]
        else:
            tab[12:13, :] = igot[1, NB:NB + 1, :]

    finish(unpack_first)

    middle_rows = (sub >= 1) & (sub <= 4)
    coarse_a = jnp.where(middle_rows, pltpu.roll(row(s2, 0), 1, 0), row(s2, 2))
    coarse_b = jnp.where(middle_rows, pltpu.roll(row(s2, 1), 1, 0), row(s2, 3))
    base = jnp.where(sub == 0, 3 * LANES, jnp.where(sub == 5, 0, (sub - 1) * LANES))
    index_c, high_c, weight_c = [], [], []
    for k in range(NB):
        p = row(nbc, k)
        low_col = pick(row(tab, 0), p & (LANES - 1)) - width
        up_col = pick(row(tab, 1), (p - (width + REACH)) & (LANES - 1)) + width
        col = jnp.where(p < REACH, low_col, jnp.where(p >= width + REACH, up_col, p - REACH))
        rel = col - base
        index_c.append(rel & (LANES - 1))
        high_c.append(rel >= LANES - REACH)
        weight_c.append(row(ewc, k))
        fine = jnp.where(sub < 4, pltpu.roll(rel, 7, 0), pltpu.roll(rel, 3, 0))
        put(idxf, k, fine)
        put(ewf, k, iced * row(ewf, k))

    def near(value, before, after, index, high, weight):
        first = jnp.where(tail, before, value)
        second = jnp.where(tail, value, after)
        acc = None
        for k in range(NB):
            got_k = jnp.where(high[k], pick(second, index[k]), pick(first, index[k]))
            term = weight[k] * got_k
            acc = term if acc is None else acc + term
        return acc

    def near_coarse(value):
        return near(
            value, pltpu.roll(value, 1, 0), pltpu.roll(value, 7, 0), index_c, high_c, weight_c
        )

    first_tile, last_tile = tile == 0, tile == 3

    def near_fine(value, halo):
        before = jnp.where(first_tile, halo, pltpu.roll(value, 1, 0))
        after = jnp.where(last_tile, halo, pltpu.roll(value, 7, 0))
        index, high, weight = [], [], []
        for k in range(NB):
            rel = row(idxf, k)
            index.append(rel & (LANES - 1))
            high.append(rel >= LANES - REACH)
            weight.append(row(ewf, k))
        return near(value, before, after, index, high, weight)

    def first_residual(l, norm):
        at = pl.ds(pl.multiple_of(8 * l, 8), 8)
        resid = w2[at, :] - near_fine(x2[at, :], h2[at, :])
        w2[at, :] = resid
        u2[0, at, :] = -resid
        return norm + resid * resid

    norm = lax.fori_loop(0, layers, first_residual, zero, unroll=True)
    for c in range(2):
        for t in range(4):
            res_out[c, :, t * LANES:(t + 1) * LANES] = gathered(w2, 4 * c + t, layers)

    def flat(value):
        return jnp.sum(value, axis=0, keepdims=True)

    def reduce_all(step, values):
        mine = red.at[step, me]
        mine[...] = jnp.concatenate(
            [flat(v) for v in values] + [jnp.zeros((8 - len(values), LANES), jnp.float32)], axis=0
        )

        def copy(peer, slot):
            return pltpu.make_async_remote_copy(
                src_ref=red.at[step, me], dst_ref=red.at[step, slot],
                send_sem=rs.at[step, peer], recv_sem=rr.at[step, slot],
                device_id={"region": peer}, device_id_type=MESH,
            )

        for off in range(1, n):
            copy(lax.rem(me + off, n), me).start()

        def finish():
            for off in range(1, n):
                peer = lax.rem(me + n - off, n)
                copy(peer, peer).wait_recv()
            total = red[step, 0]
            for slot in range(1, n):
                total = total + red[step, slot]
            for off in range(1, n):
                copy(lax.rem(me + off, n), me).wait_send()
            full = jnp.sum(total, axis=1, keepdims=True)
            return [full[i:i + 1, :] for i in range(len(values))]

        return finish

    sizes, hess, grams = [], [], []
    for j in range(M):
        uj, zj = u2.at[j], z2.at[j]
        values = [row(uj, 0) * row(inv2, 0)]
        for l in range(1, layers):
            values.append(row(uj, l) * row(inv2, l) + row(li2, l) * values[l - 1])
        solved = values[layers - 1]
        mean = zero
        for l in range(layers - 1, -1, -1):
            if l < layers - 1:
                solved = values[l] + row(pr2, l) * solved
            put(zj, l, solved)
            weighted = row(iv2, l) * solved
            put(x2, l, weighted)
            mean = mean + weighted
        put(x2, layers, mean * (1.0 / layers))
        for side, s in ((0, 0), (1, 3)):
            msg[j, side, 0:layers + 1, :] = gathered(x2, s, layers + 1)
            msg[j, side, 24:25 + layers, :] = gathered(x2, s + 4, layers + 1)
        finish = exchange([(msg.at[j], got.at[j], hs.at[j], hr.at[j])])

        def unpack(side, j=j):
            s = 0 if side == 0 else 3
            spread(h2, s, layers + 1, got[j, side, 0:layers + 1, :])
            spread(h2, s + 4, layers + 1, got[j, side, 24:25 + layers, :])

        finish(unpack)
        own, halo = row(x2, layers), row(h2, layers)
        outer = [
            jnp.where(sub == 0, halo, jnp.where(sub == 5, pltpu.roll(halo, 2, 0), 0.0)),
            jnp.where(
                sub == 0, pltpu.roll(halo, 4, 0), jnp.where(sub == 5, pltpu.roll(halo, 6, 0), 0.0)
            ),
        ]
        result = []
        for c in range(2):
            start = jnp.where(middle_rows, pltpu.roll(own, 1 if c == 0 else 5, 0), outer[c])
            source = near_coarse(start)
            corr = coarse_a * source
            for sweep in range(2):
                corr = 0.2 * corr + coarse_a * (source + near_coarse(coarse_b * corr))
            result.append(corr)
        e0, e1 = result
        corr = jnp.where(sub < 4, pltpu.roll(e0, 7, 0), pltpu.roll(e1, 3, 0))
        corr_halo = jnp.where(
            sub < 4,
            jnp.where(sub == 0, e0, pltpu.roll(e0, 6, 0)),
            jnp.where(sub == 4, pltpu.roll(e1, 4, 0), pltpu.roll(e1, 2, 0)),
        )

        def image(l, carry, j=j, uj=uj, zj=zj, corr=corr, corr_halo=corr_halo):
            at = pl.ds(pl.multiple_of(8 * l, 8), 8)
            zj[at, :] = zj[at, :] + corr
            value = x2[at, :] + iv2[at, :] * corr
            halo = h2[at, :] + ivh2[at, :] * corr_halo
            w = uj[at, :] + td2[at, :] * corr - near_fine(value, halo)
            w2[at, :] = w
            out = [carry[i] + u2[i, at, :] * w for i in range(j + 1)]
            if j == M - 1:
                out.append(carry[j + 1] + w * w)
            return tuple(out)

        count = j + 1 + (j == M - 1)
        dots = lax.fori_loop(0, layers, image, (zero,) * count, unroll=True)
        reduced = reduce_all(j, list(dots) + [norm])()
        size = jnp.sqrt(reduced[-1] + 1e-12)
        sizes.append(size)
        column = [reduced[i] / sizes[i] / size for i in range(j + 1)]
        hess.append(column)
        if j < M - 1:
            inverse = 1.0 / size
            scale = [column[i] / sizes[i] for i in range(j + 1)]
            inverse = jnp.broadcast_to(inverse, (8, LANES))
            scale = [jnp.broadcast_to(s, (8, LANES)) for s in scale]

            def next_basis(l, norm, j=j, scale=scale, inverse=inverse):
                at = pl.ds(pl.multiple_of(8 * l, 8), 8)
                fresh = w2[at, :] * inverse
                for i in range(j + 1):
                    fresh = fresh - scale[i] * u2[i, at, :]
                u2[j + 1, at, :] = fresh
                return norm + fresh * fresh

            norm = lax.fori_loop(0, layers, next_basis, zero, unroll=True)
        else:
            square = reduced[M] / size / size
            for i in range(M):
                square = square - column[i] * column[i]
            last_square = jnp.maximum(square, 0.0) + 1e-12

    def entry(i, j):
        if i <= j:
            return hess[j][i]
        return sizes[i] if i == j + 1 else None

    gram = [[None] * M for _ in range(M)]
    for a in range(M):
        for b in range(a + 1):
            acc = None
            for i in range(min(a, b) + 2):
                if i == M:
                    term = last_square
                else:
                    left, right = entry(i, a), entry(i, b)
                    if left is None or right is None:
                        continue
                    term = left * right
                acc = term if acc is None else acc + term
            gram[a][b] = acc
    right = [sizes[0] * hess[j][0] for j in range(M)]
    chol = [[None] * M for _ in range(M)]
    inv_diag = []
    for a in range(M):
        for b in range(a + 1):
            acc = gram[a][b]
            for i in range(b):
                acc = acc - chol[a][i] * chol[b][i]
            if a == b:
                root = jnp.sqrt(acc)
                inv_diag.append(1.0 / root)
            else:
                chol[a][b] = acc * inv_diag[b]
    forward = []
    for a in range(M):
        acc = right[a]
        for i in range(a):
            acc = acc - chol[a][i] * forward[i]
        forward.append(acc * inv_diag[a])
    coeffs = [None] * M
    for a in range(M - 1, -1, -1):
        acc = forward[a]
        for i in range(a + 1, M):
            acc = acc - chol[i][a] * coeffs[i]
        coeffs[a] = acc * inv_diag[a]
    coeffs = [jnp.broadcast_to(coeffs[j] / sizes[j], (8, LANES)) for j in range(M)]
    for l in range(layers):
        value = row(v2, l)
        for j in range(M):
            value = value + coeffs[j] * row(z2.at[j], l)
        put(w2, l, value)
    for c in range(2):
        for t in range(4):
            vel_out[c, :, t * LANES:(t + 1) * LANES] = gathered(w2, 4 * c + t, layers)


def body(velocity_start, forcing, rate_factor, basal_drag, edge_weight, nbr_local, send_list, ice_mask):
    n = lax.axis_size("region")
    layers = velocity_start.shape[1]
    full = 8 * layers
    f32, i32 = jnp.float32, jnp.int32
    V, D = pltpu.VMEM, pltpu.SemaphoreType.DMA
    spec = pl.BlockSpec(memory_space=pltpu.VMEM)
    shape = jax.ShapeDtypeStruct(velocity_start.shape, f32)
    field = V((full, LANES), f32)
    return tuple(pl.pallas_call(
        functools.partial(kernel, n, layers),
        out_shape=(shape, shape),
        in_specs=[spec] * 8,
        out_specs=(spec, spec),
        scratch_shapes=[
            field, field, field, field, field, field, field,
            V((full + 8, LANES), f32), V((full + 8, LANES), f32), field, field, V((32, LANES), f32),
            V((M, full, LANES), f32), V((M, full, LANES), f32),
            V((8 * NB, LANES), f32), V((8 * NB, LANES), i32),
            V((8 * NB, LANES), f32), V((8 * NB, LANES), i32), V((16, LANES), i32),
            V((M, 2, 48, LANES), f32), V((M, 2, 48, LANES), f32),
            V((2, 80, LANES), f32), V((2, 80, LANES), f32),
            V((2, 8, LANES), i32), V((2, 8, LANES), i32),
            V((M, n, 8, LANES), f32),
            D((M, 2)), D((M, 2)), D((2,)), D((2,)), D((2,)), D((2,)), D((M, n)), D((M, n)),
        ],
        compiler_params=pltpu.CompilerParams(
            collective_id=0, has_side_effects=True, vmem_limit_bytes=32 * 1024 * 1024
        ),
    )(
        velocity_start, forcing, rate_factor, basal_drag.reshape(4, LANES), edge_weight, nbr_local,
        send_list, ice_mask.reshape(4, LANES),
    ))


def solution(mesh):
    cols = P(None, None, ("ens", "region"))
    in_specs = (
        cols, cols, P(None, ("ens", "region")), P("region"), P(None, "region"), P(None, "region"),
        P(None, "region"), P("region"),
    )
    return jax.shard_map(body, mesh=mesh, in_specs=in_specs, out_specs=(cols, cols), check_vma=False)
```

time: 784 us -> 46.2 us (0.06); the launches traced: 771 us -> 46 us
  blocking collectives: 286 us -> 0 us
  local copies, waits for them, and re-layouts: 278 us -> 3.1 us
  other arithmetic: 92.6 us -> 0 us
  starting transfers between devices: 87.8 us -> 0 us
  Pallas kernels: 0 us -> 42.2 us
  matrix products: 13.8 us -> 0 us
    psum x9 -> x0, blocking collectives: 286 us -> none  [the longest x4 130 us: body(): proj = lax.psum(local_proj, 'region')]
    gather x238 -> x0, local copies, waits for them, and re-layouts: 227 us -> none  [the longest x170 172 us: near_sum(): jnp.take(extended, nbr_local[which], axis=-1)]
    ppermute x34 -> x0, starting transfers between devices: 87.8 us -> none  [the longest x17 65.9 us: with_halo(): before = lax.ppermute(last, axis, up)]
    pallas_call x0 -> x1, Pallas kernels: none -> 42.2 us  [body(): pl.pallas_call(functools.partial(kernel, n, layers), out_shape=(shape, sh...]
    another operation x29 -> x0, other arithmetic: 20 us -> none
    dot_general x8 -> x0, matrix products: 13.6 us -> none  [the longest x3 6.56 us: body(): local_proj = jnp.einsum('jabc,abc->j', stacked, image, precision=highest)]
    another operation x21 -> x0, local copies, waits for them, and re-layouts: 12.6 us -> none  [the longest x5 9.37 us: body(): stacked = jnp.stack(basis)]
    scatter x8 -> x0, local copies, waits for them, and re-layouts: 12.3 us -> none  [the longest x4 8.19 us: body(): hessen = hessen.at[:inner_step + 1, inner_step].set(proj)]
  transfers between devices with their start and end apart: 34 -> 0, of which waited for: 6 -> 0; matrix products, arithmetic and copies ran while one was open for 7% -> 0% of each run, Pallas kernels for 0% -> 0%
where the time goes in v1:
time: 46.2 us; the launch traced here: 46 us
  Pallas kernels  42.2 us (91%)
  local copies, waits for them, and re-layouts  3.1 us (7%)
  between operations  0.73 us (2%)
    pallas_call x1, Pallas kernels, body(): pl.pallas_call(functools.partial(kernel, n, layers), out_shape=(shape, sh...  42.2 us
    unnamed x16, local copies, waits for them, and re-layouts  1.7 us
    pallas_call x2, local copies, waits for them, and re-layouts, body(): pl.pallas_call(functools.partial(kernel, n, layers), out_shape=(shape, sh...  1.4 us

profile of v1, /device:TPU:0, one launch (start us, length us, event | category | flops | bytes accessed | tf_op | source)
XLA Modules:
  0.0 46.0 jit_solution(11478086216306727536)
XLA Ops:
  0.6 0.0 copy-start.6
  0.6 0.9 %copy.10.vel = f32[2,20,512]{2,1,0:T(8,128)S(1)} copy(f32[2,20,512]{2,0,1:T(2,128)} %param.8) | data formatting | bytes 163840 | tf_op args[0]
  1.6 0.0 copy-done.6
  1.6 0.0 copy-start
  1.6 0.0 copy-start.1
  1.6 0.0 copy-start.2
  1.6 0.0 copy-start.3
  1.6 0.0 copy-start.4
  1.6 0.0 copy-start.5
  1.7 0.7 %copy-done = f32[20,512]{1,0:T(8,128)S(1)} copy-done((f32[20,512]{1,0:T(8,128)S(1)}, f32[20,512]{1,0:T(8,128)}, u32[]{:S(2)}) %copy-start) | copy-done | bytes 40984
  2.4 0.0 copy-done.1
  2.4 0.0 copy-done.2
  2.4 0.0 copy-done.3
  2.4 0.0 copy-done.4
  2.4 0.0 copy-done.5
  2.4 42.2 %shard_map.95 = (f32[2,20,512]{2,1,0:T(8,128)S(1)}, f32[2,20,512]{2,1,0:T(8,128)S(1)}) custom-call(f32[2,20,512]{2,1,0:T(8,128)S(1)} %copy.10.vel, f32[2,20,512]{2,1,0:T(8,128)S(1)} %copy.11.frc, f32[20,512]{1,0:T(8,128)S(1)} %copy-done, f32[4,128]{1,0:T(4,128)S(1)} %bitcast.2, f32[6,512]{1,0:T(8,128)S(1)} %copy-done.1, s32[6,512]{1,0:T(8,128)S(1)} %copy-done.2, ...), custom_call_target="tpu_custom_call" | custom-call | tf_op jit(solution)/shard_map/pallas_call | solution.py:465
  44.6 0.7 %copy.12 = f32[2,20,512]{2,0,1:T(2,128)} copy(f32[2,20,512]{2,1,0:T(8,128)S(1)} %get-tuple-element.2) | data formatting | bytes 163840 | tf_op jit(solution)/shard_map/pallas_call | solution.py:465
  45.3 0.7 %copy.13 = f32[2,20,512]{2,0,1:T(2,128)} copy(f32[2,20,512]{2,1,0:T(8,128)S(1)} %get-tuple-element.3) | data formatting | bytes 163840 | tf_op jit(solution)/shard_map/pallas_call | solution.py:465
  (1 shorter events, 0.0 us)
Async XLA Ops:
  0.6 1.0 %copy-start.6 = (f32[2,20,512]{2,0,1:T(2,128)S(1)}, f32[2,20,512]{2,0,1:T(2,128)}, u32[]{:S(2)}) copy-start(f32[2,20,512]{2,0,1:T(2,128)} %param.9) | copy-start | bytes 245764
  1.6 0.8 %copy-start = (f32[20,512]{1,0:T(8,128)S(1)}, f32[20,512]{1,0:T(8,128)}, u32[]{:S(2)}) copy-start(f32[20,512]{1,0:T(8,128)} %rate.1) | copy-start | bytes 122884
  1.6 0.8 %copy-start.1 = (f32[6,512]{1,0:T(8,128)S(1)}, f32[6,512]{1,0:T(8,128)}, u32[]{:S(2)}) copy-start(f32[6,512]{1,0:T(8,128)} %ew.1) | copy-start | bytes 36868
  1.6 0.8 %copy-start.2 = (s32[6,512]{1,0:T(8,128)S(1)}, s32[6,512]{1,0:T(8,128)}, u32[]{:S(2)}) copy-start(s32[6,512]{1,0:T(8,128)} %nbr.1) | copy-start | bytes 36868
  1.6 0.8 %copy-start.3 = (f32[512]{0:T(512)S(1)}, f32[512]{0:T(512)}, u32[]{:S(2)}) copy-start(f32[512]{0:T(512)} %param.11) | copy-start | bytes 6148
  1.6 0.8 %copy-start.4 = (s32[512]{0:T(512)S(1)}, s32[512]{0:T(512)}, u32[]{:S(2)}) copy-start(s32[512]{0:T(512)} %param.15) | copy-start | bytes 6148
  1.6 0.8 %copy-start.5 = (s32[2,32]{1,0:T(2,128)S(1)}, s32[2,32]{1,0:T(2,128)}, u32[]{:S(2)}) copy-start(s32[2,32]{1,0:T(2,128)} %send.1) | copy-start | bytes 772

commit v2 on v1

--- a/solution.py
+++ b/solution.py
@@ -19,11 +19,11 @@
 
 
 def kernel(
-    n, layers,
+    n, inner, layers,
     vel, frc, rate, drag, ew, nbr, send, mask, vel_out, res_out,
-    v2, f2, iv2, inv2, li2, pr2, td2, x2, h2, ivh2, w2, s2, u2, z2, ewf, idxf, ewc, nbc, tab,
-    msg, got, smsg, sgot, imsg, igot, red,
-    hs, hr, ss, sr, is_, ir, rs, rr,
+    v2, f2, iv2, inv2, li2, pr2, td2, x2, h2, ivh2, w2, s2, u2, z2, q2, g2, ewf, idxf, ewc, nbc, tab,
+    msg, got, smsg, sgot, imsg, igot, red0, red1,
+    hs, hr, ss, sr, is_, ir, rs0, rr0, rs1, rr1,
 ):
     me = lax.axis_index("region")
     barrier = pltpu.get_barrier_semaphore()
@@ -278,39 +278,91 @@
     def flat(value):
         return jnp.sum(value, axis=0, keepdims=True)
 
-    def reduce_all(step, values):
-        mine = red.at[step, me]
-        mine[...] = jnp.concatenate(
-            [flat(v) for v in values] + [jnp.zeros((8 - len(values), LANES), jnp.float32)], axis=0
-        )
-
-        def copy(peer, slot):
-            return pltpu.make_async_remote_copy(
-                src_ref=red.at[step, me], dst_ref=red.at[step, slot],
-                send_sem=rs.at[step, peer], recv_sem=rr.at[step, slot],
+    ia, ib = lax.rem(me, inner), lax.div(me, inner)
+
+    def partner(phase, off):
+        if phase == 0:
+            spot = lax.rem(ia + off, inner)
+            return spot, ib * inner + spot
+        spot = lax.rem(ib + off, n // inner)
+        return spot, spot * inner + ia
+
+    reds = ((red0, rs0, rr0, inner, ia), (red1, rs1, rr1, n // inner, ib))
+
+    def phase_start(phase, step, tile_value):
+        red, rs, rr, group, mine = reds[phase]
+        red[step, mine] = tile_value
+        for off in range(1, group):
+            spot, peer = partner(phase, off)
+            pltpu.make_async_remote_copy(
+                src_ref=red.at[step, mine], dst_ref=red.at[step, mine],
+                send_sem=rs.at[step, spot], recv_sem=rr.at[step, mine],
                 device_id={"region": peer}, device_id_type=MESH,
-            )
-
-        for off in range(1, n):
-            copy(lax.rem(me + off, n), me).start()
-
-        def finish():
-            for off in range(1, n):
-                peer = lax.rem(me + n - off, n)
-                copy(peer, peer).wait_recv()
-            total = red[step, 0]
-            for slot in range(1, n):
-                total = total + red[step, slot]
-            for off in range(1, n):
-                copy(lax.rem(me + off, n), me).wait_send()
-            full = jnp.sum(total, axis=1, keepdims=True)
-            return [full[i:i + 1, :] for i in range(len(values))]
-
-        return finish
-
-    sizes, hess, grams = [], [], []
+            ).start()
+
+    def phase_end(phase, step):
+        red, rs, rr, group, mine = reds[phase]
+        copies = []
+        for off in range(1, group):
+            spot, peer = partner(phase, off)
+            copies.append(pltpu.make_async_remote_copy(
+                src_ref=red.at[step, mine], dst_ref=red.at[step, spot],
+                send_sem=rs.at[step, spot], recv_sem=rr.at[step, spot],
+                device_id={"region": peer}, device_id_type=MESH,
+            ))
+        for copy in copies:
+            copy.wait_recv()
+        total = red[step, 0]
+        for slot in range(1, group):
+            total = total + red[step, slot]
+        for copy in copies:
+            copy.wait_send()
+        return total
+
+    def reduce_start(step, values):
+        blank = jnp.zeros((8 - len(values), LANES), jnp.float32)
+        phase_start(0, step, jnp.concatenate([flat(v) for v in values] + [blank], axis=0))
+
+    def reduce_middle(step):
+        phase_start(1, step, phase_end(0, step))
+
+    def reduce_end(step):
+        full = jnp.sum(phase_end(1, step), axis=1, keepdims=True)
+        return [full[i:i + 1, :] for i in range(8)]
+
+    def wide(value):
+        return jnp.broadcast_to(value, (8, LANES))
+
+    def layer_rows(l):
+        return pl.ds(pl.multiple_of(8 * l, 8), 8)
+
+    def mix(ref, j, scale, shifts, at):
+        out = scale * ref[j, at, :]
+        for i in range(j):
+            out = out + shifts[i] * ref[i, at, :]
+        return out
+
+    def settle(j):
+        sums = reduce_end(j)
+        size = jnp.sqrt(sums[j + 1] + 1e-12)
+        sizes.append(size)
+        hess.append([sums[i] / sizes[i] / size for i in range(j + 1)])
+        return sums
+
+    def mix_directions(j):
+        scale, shifts = mixes[j]
+
+        def one(l, carry):
+            at = layer_rows(l)
+            z2[j, at, :] = mix(z2, j, scale, shifts, at)
+            return carry
+
+        lax.fori_loop(0, layers, one, 0, unroll=True)
+
+    mixes = {}
+    sizes, hess = [], []
     for j in range(M):
-        uj, zj = u2.at[j], z2.at[j]
+        uj, zj = (u2.at[0] if j == 0 else g2), z2.at[j]
         values = [row(uj, 0) * row(inv2, 0)]
         for l in range(1, layers):
             values.append(row(uj, l) * row(inv2, l) + row(li2, l) * values[l - 1])
@@ -334,6 +386,10 @@
             spread(h2, s, layers + 1, got[j, side, 0:layers + 1, :])
             spread(h2, s + 4, layers + 1, got[j, side, 24:25 + layers, :])
 
+        if j >= 2:
+            mix_directions(j - 1)
+        if j >= 1:
+            reduce_middle(j - 1)
         finish(unpack)
         own, halo = row(x2, layers), row(h2, layers)
         outer = [
@@ -359,44 +415,54 @@
         )
 
         def image(l, carry, j=j, uj=uj, zj=zj, corr=corr, corr_halo=corr_halo):
-            at = pl.ds(pl.multiple_of(8 * l, 8), 8)
+            at = layer_rows(l)
             zj[at, :] = zj[at, :] + corr
             value = x2[at, :] + iv2[at, :] * corr
             halo = h2[at, :] + ivh2[at, :] * corr_halo
             w = uj[at, :] + td2[at, :] * corr - near_fine(value, halo)
-            w2[at, :] = w
-            out = [carry[i] + u2[i, at, :] * w for i in range(j + 1)]
-            if j == M - 1:
-                out.append(carry[j + 1] + w * w)
-            return tuple(out)
-
-        count = j + 1 + (j == M - 1)
-        dots = lax.fori_loop(0, layers, image, (zero,) * count, unroll=True)
-        reduced = reduce_all(j, list(dots) + [norm])()
-        size = jnp.sqrt(reduced[-1] + 1e-12)
-        sizes.append(size)
-        column = [reduced[i] / sizes[i] / size for i in range(j + 1)]
-        hess.append(column)
-        if j < M - 1:
-            inverse = 1.0 / size
-            scale = [column[i] / sizes[i] for i in range(j + 1)]
-            inverse = jnp.broadcast_to(inverse, (8, LANES))
-            scale = [jnp.broadcast_to(s, (8, LANES)) for s in scale]
-
-            def next_basis(l, norm, j=j, scale=scale, inverse=inverse):
-                at = pl.ds(pl.multiple_of(8 * l, 8), 8)
-                fresh = w2[at, :] * inverse
-                for i in range(j + 1):
-                    fresh = fresh - scale[i] * u2[i, at, :]
-                u2[j + 1, at, :] = fresh
-                return norm + fresh * fresh
-
-            norm = lax.fori_loop(0, layers, next_basis, zero, unroll=True)
+            q2[j, at, :] = w
+            if j > 0:
+                return carry
+            g2[at, :] = w - uj[at, :]
+            return (carry[0] + uj[at, :] * w,)
+
+        dots = lax.fori_loop(0, layers, image, (zero,), unroll=True)
+        if j == 0:
+            dots = dots + (norm,)
         else:
-            square = reduced[M] / size / size
-            for i in range(M):
-                square = square - column[i] * column[i]
-            last_square = jnp.maximum(square, 0.0) + 1e-12
+            settle(j - 1)
+            size, column = sizes[j - 1], hess[j - 1]
+            shifts = [wide(-column[i] / sizes[i]) for i in range(j - 1)]
+            shifts.append(wide((1.0 - column[j - 1]) / size))
+            scale = wide(1.0 / size)
+            mixes[j] = (scale, shifts)
+
+            def orthogonal(l, carry, j=j, scale=scale, shifts=shifts):
+                at = layer_rows(l)
+                u = scale * g2[at, :]
+                for i in range(j):
+                    u = u + shifts[i] * u2[i, at, :]
+                w = mix(q2, j, scale, shifts, at)
+                if j < M - 1:
+                    u2[j, at, :] = u
+                    q2[j, at, :] = w
+                    g2[at, :] = w - u
+                out = [carry[i] + u2[i, at, :] * w for i in range(j)]
+                out += [carry[j] + u * w, carry[j + 1] + u * u]
+                if j == M - 1:
+                    out.append(carry[j + 2] + w * w)
+                return tuple(out)
+
+            dots = lax.fori_loop(
+                0, layers, orthogonal, (zero,) * (j + 2 + (j == M - 1)), unroll=True
+            )
+        reduce_start(j, list(dots))
+    mix_directions(M - 1)
+    reduce_middle(M - 1)
+    square = settle(M - 1)[M + 1] / sizes[M - 1] / sizes[M - 1]
+    for i in range(M):
+        square = square - hess[M - 1][i] * hess[M - 1][i]
+    last_square = jnp.maximum(square, 0.0) + 1e-12
 
     def entry(i, j):
         if i <= j:
@@ -457,27 +523,29 @@
     n = lax.axis_size("region")
     layers = velocity_start.shape[1]
     full = 8 * layers
+    inner = max(g for g in range(1, n + 1) if n % g == 0 and g * g <= n)
     f32, i32 = jnp.float32, jnp.int32
     V, D = pltpu.VMEM, pltpu.SemaphoreType.DMA
     spec = pl.BlockSpec(memory_space=pltpu.VMEM)
     shape = jax.ShapeDtypeStruct(velocity_start.shape, f32)
     field = V((full, LANES), f32)
     return tuple(pl.pallas_call(
-        functools.partial(kernel, n, layers),
+        functools.partial(kernel, n, inner, layers),
         out_shape=(shape, shape),
         in_specs=[spec] * 8,
         out_specs=(spec, spec),
         scratch_shapes=[
             field, field, field, field, field, field, field,
             V((full + 8, LANES), f32), V((full + 8, LANES), f32), field, field, V((32, LANES), f32),
-            V((M, full, LANES), f32), V((M, full, LANES), f32),
+            V((M, full, LANES), f32), V((M, full, LANES), f32), V((M, full, LANES), f32), field,
             V((8 * NB, LANES), f32), V((8 * NB, LANES), i32),
             V((8 * NB, LANES), f32), V((8 * NB, LANES), i32), V((16, LANES), i32),
             V((M, 2, 48, LANES), f32), V((M, 2, 48, LANES), f32),
             V((2, 80, LANES), f32), V((2, 80, LANES), f32),
             V((2, 8, LANES), i32), V((2, 8, LANES), i32),
-            V((M, n, 8, LANES), f32),
-            D((M, 2)), D((M, 2)), D((2,)), D((2,)), D((2,)), D((2,)), D((M, n)), D((M, n)),
+            V((M, inner, 8, LANES), f32), V((M, n // inner, 8, LANES), f32),
+            D((M, 2)), D((M, 2)), D((2,)), D((2,)), D((2,)), D((2,)), D((M, inner)), D((M, inner)),
+            D((M, n // inner)), D((M, n // inner)),
         ],
         compiler_params=pltpu.CompilerParams(
             collective_id=0, has_side_effects=True, vmem_limit_bytes=32 * 1024 * 1024

time: 46.2 us -> 43.1 us (0.933)
  Pallas kernels: 42.2 us -> 39 us
    pallas_call x1, Pallas kernels: 42.2 us -> 39 us  [body(): pl.pallas_call(functools.partial(kernel, n, inner, layers), out_shape=(sh...]
where the time goes in v2:
time: 43.1 us; the launch traced here: 42.9 us
  Pallas kernels  39 us (90%)
  local copies, waits for them, and re-layouts  3.1 us (7%)
  between operations  0.73 us (2%)
    pallas_call x1, Pallas kernels, body(): pl.pallas_call(functools.partial(kernel, n, inner, layers), out_shape=(sh...  39 us
    unnamed x16, local copies, waits for them, and re-layouts  1.7 us
    pallas_call x2, local copies, waits for them, and re-layouts, body(): pl.pallas_call(functools.partial(kernel, n, inner, layers), out_shape=(sh...  1.4 us

profile of v2, /device:TPU:0, one launch (start us, length us, event | category | flops | bytes accessed | tf_op | source)
XLA Modules:
  0.0 42.9 jit_solution(18034963180093533078)
XLA Ops:
  0.6 0.0 copy-start.6
  0.6 0.9 %copy.10.vel = f32[2,20,512]{2,1,0:T(8,128)S(1)} copy(f32[2,20,512]{2,0,1:T(2,128)} %param.8) | data formatting | bytes 163840 | tf_op args[0]
  1.6 0.0 copy-done.6
  1.6 0.0 copy-start
  1.6 0.0 copy-start.1
  1.6 0.0 copy-start.2
  1.6 0.0 copy-start.3
  1.6 0.0 copy-start.4
  1.6 0.0 copy-start.5
  1.7 0.7 %copy-done = f32[20,512]{1,0:T(8,128)S(1)} copy-done((f32[20,512]{1,0:T(8,128)S(1)}, f32[20,512]{1,0:T(8,128)}, u32[]{:S(2)}) %copy-start) | copy-done | bytes 40984
  2.4 0.0 copy-done.1
  2.4 0.0 copy-done.2
  2.4 0.0 copy-done.3
  2.4 0.0 copy-done.4
  2.4 0.0 copy-done.5
  2.4 39.0 %shard_map.95 = (f32[2,20,512]{2,1,0:T(8,128)S(1)}, f32[2,20,512]{2,1,0:T(8,128)S(1)}) custom-call(f32[2,20,512]{2,1,0:T(8,128)S(1)} %copy.10.vel, f32[2,20,512]{2,1,0:T(8,128)S(1)} %copy.11.frc, f32[20,512]{1,0:T(8,128)S(1)} %copy-done, f32[4,128]{1,0:T(4,128)S(1)} %bitcast.2, f32[6,512]{1,0:T(8,128)S(1)} %copy-done.1, s32[6,512]{1,0:T(8,128)S(1)} %copy-done.2, ...), custom_call_target="tpu_custom_call" | custom-call | tf_op jit(solution)/shard_map/pallas_call | solution.py:532
  41.5 0.7 %copy.12 = f32[2,20,512]{2,0,1:T(2,128)} copy(f32[2,20,512]{2,1,0:T(8,128)S(1)} %get-tuple-element.2) | data formatting | bytes 163840 | tf_op jit(solution)/shard_map/pallas_call | solution.py:532
  42.2 0.7 %copy.13 = f32[2,20,512]{2,0,1:T(2,128)} copy(f32[2,20,512]{2,1,0:T(8,128)S(1)} %get-tuple-element.3) | data formatting | bytes 163840 | tf_op jit(solution)/shard_map/pallas_call | solution.py:532
  (1 shorter events, 0.0 us)
Async XLA Ops:
  0.6 1.0 %copy-start.6 = (f32[2,20,512]{2,0,1:T(2,128)S(1)}, f32[2,20,512]{2,0,1:T(2,128)}, u32[]{:S(2)}) copy-start(f32[2,20,512]{2,0,1:T(2,128)} %param.9) | copy-start | bytes 245764
  1.6 0.8 %copy-start = (f32[20,512]{1,0:T(8,128)S(1)}, f32[20,512]{1,0:T(8,128)}, u32[]{:S(2)}) copy-start(f32[20,512]{1,0:T(8,128)} %rate.1) | copy-start | bytes 122884
  1.6 0.8 %copy-start.1 = (f32[6,512]{1,0:T(8,128)S(1)}, f32[6,512]{1,0:T(8,128)}, u32[]{:S(2)}) copy-start(f32[6,512]{1,0:T(8,128)} %ew.1) | copy-start | bytes 36868
  1.6 0.8 %copy-start.2 = (s32[6,512]{1,0:T(8,128)S(1)}, s32[6,512]{1,0:T(8,128)}, u32[]{:S(2)}) copy-start(s32[6,512]{1,0:T(8,128)} %nbr.1) | copy-start | bytes 36868
  1.6 0.8 %copy-start.3 = (f32[512]{0:T(512)S(1)}, f32[512]{0:T(512)}, u32[]{:S(2)}) copy-start(f32[512]{0:T(512)} %param.11) | copy-start | bytes 6148
  1.6 0.8 %copy-start.4 = (s32[512]{0:T(512)S(1)}, s32[512]{0:T(512)}, u32[]{:S(2)}) copy-start(s32[512]{0:T(512)} %param.15) | copy-start | bytes 6148
  1.6 0.8 %copy-start.5 = (s32[2,32]{1,0:T(2,128)S(1)}, s32[2,32]{1,0:T(2,128)}, u32[]{:S(2)}) copy-start(s32[2,32]{1,0:T(2,128)} %send.1) | copy-start | bytes 772

commit v3 on v1

--- a/solution.py
+++ b/solution.py
@@ -19,19 +19,42 @@
 
 
 def kernel(
-    n, layers,
+    n, inner, layers,
     vel, frc, rate, drag, ew, nbr, send, mask, vel_out, res_out,
     v2, f2, iv2, inv2, li2, pr2, td2, x2, h2, ivh2, w2, s2, u2, z2, ewf, idxf, ewc, nbc, tab,
-    msg, got, smsg, sgot, imsg, igot, red,
-    hs, hr, ss, sr, is_, ir, rs, rr,
+    msg, got, smsg, sgot, imsg, igot, red0, red1,
+    hs, hr, ss, sr, is_, ir, rs0, rr0, rs1, rr1,
 ):
     me = lax.axis_index("region")
     barrier = pltpu.get_barrier_semaphore()
-    for off in range(1, n):
-        pl.semaphore_signal(
-            barrier, inc=1, device_id={"region": lax.rem(me + off, n)}, device_id_type=MESH
-        )
+    ia, ib = lax.rem(me, inner), lax.div(me, inner)
     has_low, has_up = me > 0, me < n - 1
+
+    def partner(phase, off):
+        if phase == 0:
+            spot = lax.rem(ia + off, inner)
+            return spot, ib * inner + spot
+        spot = lax.rem(ib + off, n // inner)
+        return spot, spot * inner + ia
+
+    def greet(peer):
+        pl.semaphore_signal(barrier, inc=1, device_id={"region": peer}, device_id_type=MESH)
+
+    for phase, group in ((0, inner), (1, n // inner)):
+        for off in range(1, group):
+            greet(partner(phase, off)[1])
+    far_low = has_low & (ia == 0)
+    far_up = has_up & (ia == inner - 1)
+
+    @pl.when(far_low)
+    def _():
+        greet(me - 1)
+
+    @pl.when(far_up)
+    def _():
+        greet(me + 1)
+
+    greeters = (inner - 1) + (n // inner - 1) + far_low.astype(jnp.int32) + far_up.astype(jnp.int32)
     sub = lax.broadcasted_iota(jnp.int32, (8, LANES), 0)
     lane = lax.broadcasted_iota(jnp.int32, (8, LANES), 1)
     tile = sub & 3
@@ -190,7 +213,7 @@
 
         return finish
 
-    pl.semaphore_wait(barrier, n - 1)
+    pl.semaphore_wait(barrier, greeters)
     finish = exchange([(imsg, igot, is_, ir), (smsg, sgot, ss, sr)])
     put(tab, 0, jnp.full((8, LANES), width - REACH, jnp.int32))
     put(tab, 1, jnp.zeros((8, LANES), jnp.int32))
@@ -278,37 +301,45 @@
     def flat(value):
         return jnp.sum(value, axis=0, keepdims=True)
 
-    def reduce_all(step, values):
-        mine = red.at[step, me]
-        mine[...] = jnp.concatenate(
-            [flat(v) for v in values] + [jnp.zeros((8 - len(values), LANES), jnp.float32)], axis=0
-        )
-
-        def copy(peer, slot):
-            return pltpu.make_async_remote_copy(
-                src_ref=red.at[step, me], dst_ref=red.at[step, slot],
-                send_sem=rs.at[step, peer], recv_sem=rr.at[step, slot],
+    reds = ((red0, rs0, rr0, inner, ia), (red1, rs1, rr1, n // inner, ib))
+
+    def phase_start(phase, tile_value):
+        red, rs, rr, group, mine = reds[phase]
+        red[mine] = tile_value
+        for off in range(1, group):
+            spot, peer = partner(phase, off)
+            pltpu.make_async_remote_copy(
+                src_ref=red.at[mine], dst_ref=red.at[mine],
+                send_sem=rs.at[spot], recv_sem=rr.at[mine],
                 device_id={"region": peer}, device_id_type=MESH,
-            )
-
-        for off in range(1, n):
-            copy(lax.rem(me + off, n), me).start()
-
-        def finish():
-            for off in range(1, n):
-                peer = lax.rem(me + n - off, n)
-                copy(peer, peer).wait_recv()
-            total = red[step, 0]
-            for slot in range(1, n):
-                total = total + red[step, slot]
-            for off in range(1, n):
-                copy(lax.rem(me + off, n), me).wait_send()
-            full = jnp.sum(total, axis=1, keepdims=True)
-            return [full[i:i + 1, :] for i in range(len(values))]
-
-        return finish
-
-    sizes, hess, grams = [], [], []
+            ).start()
+
+    def phase_end(phase):
+        red, rs, rr, group, mine = reds[phase]
+        copies = []
+        for off in range(1, group):
+            spot, peer = partner(phase, off)
+            copies.append(pltpu.make_async_remote_copy(
+                src_ref=red.at[mine], dst_ref=red.at[spot],
+                send_sem=rs.at[spot], recv_sem=rr.at[spot],
+                device_id={"region": peer}, device_id_type=MESH,
+            ))
+        for copy in copies:
+            copy.wait_recv()
+        total = red[0]
+        for slot in range(1, group):
+            total = total + red[slot]
+        for copy in copies:
+            copy.wait_send()
+        return total
+
+    def wide(value):
+        return jnp.broadcast_to(value, (8, LANES))
+
+    def layer_rows(l):
+        return pl.ds(pl.multiple_of(8 * l, 8), 8)
+
+    products = {(0, 0): norm}
     for j in range(M):
         uj, zj = u2.at[j], z2.at[j]
         values = [row(uj, 0) * row(inv2, 0)]
@@ -359,44 +390,54 @@
         )
 
         def image(l, carry, j=j, uj=uj, zj=zj, corr=corr, corr_halo=corr_halo):
-            at = pl.ds(pl.multiple_of(8 * l, 8), 8)
+            at = layer_rows(l)
             zj[at, :] = zj[at, :] + corr
             value = x2[at, :] + iv2[at, :] * corr
             halo = h2[at, :] + ivh2[at, :] * corr_halo
             w = uj[at, :] + td2[at, :] * corr - near_fine(value, halo)
-            w2[at, :] = w
-            out = [carry[i] + u2[i, at, :] * w for i in range(j + 1)]
-            if j == M - 1:
-                out.append(carry[j + 1] + w * w)
-            return tuple(out)
-
-        count = j + 1 + (j == M - 1)
-        dots = lax.fori_loop(0, layers, image, (zero,) * count, unroll=True)
-        reduced = reduce_all(j, list(dots) + [norm])()
-        size = jnp.sqrt(reduced[-1] + 1e-12)
-        sizes.append(size)
-        column = [reduced[i] / sizes[i] / size for i in range(j + 1)]
+            fresh = w - uj[at, :]
+            if j < M - 1:
+                u2[j + 1, at, :] = fresh
+            out = [carry[i] + u2[i, at, :] * fresh for i in range(j + 1)]
+            return tuple(out) + (carry[j + 1] + fresh * fresh,)
+
+        dots = lax.fori_loop(0, layers, image, (zero,) * (j + 2), unroll=True)
+        for i in range(j + 2):
+            products[i, j + 1] = dots[i]
+
+    pairs = sorted(products)
+    tiles = [flat(products[pair]) for pair in pairs] + [jnp.zeros((1, LANES), jnp.float32)]
+    phase_start(0, jnp.concatenate(tiles, axis=0))
+    phase_start(1, phase_end(0))
+    full = jnp.sum(phase_end(1), axis=1, keepdims=True)
+    sums = {pair: full[i:i + 1, :] for i, pair in enumerate(pairs)}
+    gram_cols = []
+    for k in range(M + 1):
+        col = zero
+        for i in range(M + 1):
+            col = jnp.where(sub == i, wide(sums[min(i, k), max(i, k)]), col)
+        gram_cols.append(col)
+
+    def weigh(vector, count):
+        out = gram_cols[0] * vector[0:1, :]
+        for k in range(1, count):
+            out = out + gram_cols[k] * vector[k:k + 1, :]
+        return out
+
+    sizes = [jnp.sqrt(wide(sums[0, 0]) + 1e-12)]
+    hess = []
+    vectors = [jnp.where(sub == 0, 1.0 / sizes[0], 0.0)]
+    for j in range(M):
+        image_c = vectors[j] + pltpu.roll(vectors[j], 1, 0)
+        weighed = weigh(image_c, j + 2)
+        column = [wide(flat(vectors[i] * weighed)) for i in range(j + 1)]
+        for i in range(j + 1):
+            image_c = image_c - column[i] * vectors[i]
+        square = wide(flat(image_c * weigh(image_c, j + 2)))
+        length = jnp.sqrt(jnp.maximum(square, 0.0) + 1e-12)
         hess.append(column)
-        if j < M - 1:
-            inverse = 1.0 / size
-            scale = [column[i] / sizes[i] for i in range(j + 1)]
-            inverse = jnp.broadcast_to(inverse, (8, LANES))
-            scale = [jnp.broadcast_to(s, (8, LANES)) for s in scale]
-
-            def next_basis(l, norm, j=j, scale=scale, inverse=inverse):
-                at = pl.ds(pl.multiple_of(8 * l, 8), 8)
-                fresh = w2[at, :] * inverse
-                for i in range(j + 1):
-                    fresh = fresh - scale[i] * u2[i, at, :]
-                u2[j + 1, at, :] = fresh
-                return norm + fresh * fresh
-
-            norm = lax.fori_loop(0, layers, next_basis, zero, unroll=True)
-        else:
-            square = reduced[M] / size / size
-            for i in range(M):
-                square = square - column[i] * column[i]
-            last_square = jnp.maximum(square, 0.0) + 1e-12
+        sizes.append(length)
+        vectors.append(image_c / length)
 
     def entry(i, j):
         if i <= j:
@@ -408,13 +449,10 @@
         for b in range(a + 1):
             acc = None
             for i in range(min(a, b) + 2):
-                if i == M:
-                    term = last_square
-                else:
-                    left, right = entry(i, a), entry(i, b)
-                    if left is None or right is None:
-                        continue
-                    term = left * right
+                left, right = entry(i, a), entry(i, b)
+                if left is None or right is None:
+                    continue
+                term = left * right
                 acc = term if acc is None else acc + term
             gram[a][b] = acc
     right = [sizes[0] * hess[j][0] for j in range(M)]
@@ -442,7 +480,10 @@
         for i in range(a + 1, M):
             acc = acc - chol[i][a] * coeffs[i]
         coeffs[a] = acc * inv_diag[a]
-    coeffs = [jnp.broadcast_to(coeffs[j] / sizes[j], (8, LANES)) for j in range(M)]
+    combined = coeffs[0] * vectors[0]
+    for j in range(1, M):
+        combined = combined + coeffs[j] * vectors[j]
+    coeffs = [wide(combined[j:j + 1, :]) for j in range(M)]
     for l in range(layers):
         value = row(v2, l)
         for j in range(M):
@@ -457,13 +498,14 @@
     n = lax.axis_size("region")
     layers = velocity_start.shape[1]
     full = 8 * layers
+    inner = max(g for g in range(1, n + 1) if n % g == 0 and g * g <= n)
     f32, i32 = jnp.float32, jnp.int32
     V, D = pltpu.VMEM, pltpu.SemaphoreType.DMA
     spec = pl.BlockSpec(memory_space=pltpu.VMEM)
     shape = jax.ShapeDtypeStruct(velocity_start.shape, f32)
     field = V((full, LANES), f32)
     return tuple(pl.pallas_call(
-        functools.partial(kernel, n, layers),
+        functools.partial(kernel, n, inner, layers),
         out_shape=(shape, shape),
         in_specs=[spec] * 8,
         out_specs=(spec, spec),
@@ -476,8 +518,9 @@
             V((M, 2, 48, LANES), f32), V((M, 2, 48, LANES), f32),
             V((2, 80, LANES), f32), V((2, 80, LANES), f32),
             V((2, 8, LANES), i32), V((2, 8, LANES), i32),
-            V((M, n, 8, LANES), f32),
-            D((M, 2)), D((M, 2)), D((2,)), D((2,)), D((2,)), D((2,)), D((M, n)), D((M, n)),
+            V((inner, 16, LANES), f32), V((n // inner, 16, LANES), f32),
+            D((M, 2)), D((M, 2)), D((2,)), D((2,)), D((2,)), D((2,)), D((inner,)), D((inner,)),
+            D((n // inner,)), D((n // inner,)),
         ],
         compiler_params=pltpu.CompilerParams(
             collective_id=0, has_side_effects=True, vmem_limit_bytes=32 * 1024 * 1024

time: 46.2 us -> 34.2 us (0.74)
  Pallas kernels: 42.2 us -> 30.1 us
    pallas_call x1, Pallas kernels: 42.2 us -> 30.1 us  [body(): pl.pallas_call(functools.partial(kernel, n, inner, layers), out_shape=(sh...]
where the time goes in v3:
time: 34.2 us; the launch traced here: 34 us
  Pallas kernels  30.1 us (88%)
  local copies, waits for them, and re-layouts  3.1 us (9%)
  between operations  0.73 us (2%)
    pallas_call x1, Pallas kernels, body(): pl.pallas_call(functools.partial(kernel, n, inner, layers), out_shape=(sh...  30.1 us
    unnamed x16, local copies, waits for them, and re-layouts  1.7 us
    pallas_call x2, local copies, waits for them, and re-layouts, body(): pl.pallas_call(functools.partial(kernel, n, inner, layers), out_shape=(sh...  1.4 us

profile of v3, /device:TPU:0, one launch (start us, length us, event | category | flops | bytes accessed | tf_op | source)
XLA Modules:
  0.0 34.0 jit_solution(5799703028693983186)
XLA Ops:
  0.6 0.0 copy-start.6
  0.6 0.9 %copy.10.vel = f32[2,20,512]{2,1,0:T(8,128)S(1)} copy(f32[2,20,512]{2,0,1:T(2,128)} %param.8) | data formatting | bytes 163840 | tf_op args[0]
  1.6 0.0 copy-done.6
  1.6 0.0 copy-start
  1.6 0.0 copy-start.1
  1.6 0.0 copy-start.2
  1.6 0.0 copy-start.3
  1.6 0.0 copy-start.4
  1.6 0.0 copy-start.5
  1.7 0.7 %copy-done = f32[20,512]{1,0:T(8,128)S(1)} copy-done((f32[20,512]{1,0:T(8,128)S(1)}, f32[20,512]{1,0:T(8,128)}, u32[]{:S(2)}) %copy-start) | copy-done | bytes 40984
  2.4 0.0 copy-done.1
  2.4 0.0 copy-done.2
  2.4 0.0 copy-done.3
  2.4 0.0 copy-done.4
  2.4 0.0 copy-done.5
  2.4 30.1 %shard_map.95 = (f32[2,20,512]{2,1,0:T(8,128)S(1)}, f32[2,20,512]{2,1,0:T(8,128)S(1)}) custom-call(f32[2,20,512]{2,1,0:T(8,128)S(1)} %copy.10.vel, f32[2,20,512]{2,1,0:T(8,128)S(1)} %copy.11.frc, f32[20,512]{1,0:T(8,128)S(1)} %copy-done, f32[4,128]{1,0:T(4,128)S(1)} %bitcast.2, f32[6,512]{1,0:T(8,128)S(1)} %copy-done.1, s32[6,512]{1,0:T(8,128)S(1)} %copy-done.2, ...), custom_call_target="tpu_custom_call" | custom-call | tf_op jit(solution)/shard_map/pallas_call | solution.py:507
  32.6 0.7 %copy.12 = f32[2,20,512]{2,0,1:T(2,128)} copy(f32[2,20,512]{2,1,0:T(8,128)S(1)} %get-tuple-element.2) | data formatting | bytes 163840 | tf_op jit(solution)/shard_map/pallas_call | solution.py:507
  33.3 0.7 %copy.13 = f32[2,20,512]{2,0,1:T(2,128)} copy(f32[2,20,512]{2,1,0:T(8,128)S(1)} %get-tuple-element.3) | data formatting | bytes 163840 | tf_op jit(solution)/shard_map/pallas_call | solution.py:507
  (1 shorter events, 0.0 us)
Async XLA Ops:
  0.6 1.0 %copy-start.6 = (f32[2,20,512]{2,0,1:T(2,128)S(1)}, f32[2,20,512]{2,0,1:T(2,128)}, u32[]{:S(2)}) copy-start(f32[2,20,512]{2,0,1:T(2,128)} %param.9) | copy-start | bytes 245764
  1.6 0.8 %copy-start = (f32[20,512]{1,0:T(8,128)S(1)}, f32[20,512]{1,0:T(8,128)}, u32[]{:S(2)}) copy-start(f32[20,512]{1,0:T(8,128)} %rate.1) | copy-start | bytes 122884
  1.6 0.8 %copy-start.1 = (f32[6,512]{1,0:T(8,128)S(1)}, f32[6,512]{1,0:T(8,128)}, u32[]{:S(2)}) copy-start(f32[6,512]{1,0:T(8,128)} %ew.1) | copy-start | bytes 36868
  1.6 0.8 %copy-start.2 = (s32[6,512]{1,0:T(8,128)S(1)}, s32[6,512]{1,0:T(8,128)}, u32[]{:S(2)}) copy-start(s32[6,512]{1,0:T(8,128)} %nbr.1) | copy-start | bytes 36868
  1.6 0.8 %copy-start.3 = (f32[512]{0:T(512)S(1)}, f32[512]{0:T(512)}, u32[]{:S(2)}) copy-start(f32[512]{0:T(512)} %param.11) | copy-start | bytes 6148
  1.6 0.8 %copy-start.4 = (s32[512]{0:T(512)S(1)}, s32[512]{0:T(512)}, u32[]{:S(2)}) copy-start(s32[512]{0:T(512)} %param.15) | copy-start | bytes 6148
  1.6 0.8 %copy-start.5 = (s32[2,32]{1,0:T(2,128)S(1)}, s32[2,32]{1,0:T(2,128)}, u32[]{:S(2)}) copy-start(s32[2,32]{1,0:T(2,128)} %send.1) | copy-start | bytes 772
